TPU v7x, 32 devices: a whole 2x2x4 slice. The times are simulated.
32 devices in a mesh: groups: 2 (over y), aux: 8 (over z, x), occ: 1, vir: 2 (over core).
Axes of the slice: x: 2, y: 2, z: 4, core: 2. Of those that a mesh axis runs over, the one named last changes fastest.
Arguments:
- integrals: bfloat16 [2496, 16, 512], P(('aux', 'occ'), 'groups', 'vir'), parts along dimension 1, may hold values from -0.59765625 to 0.59765625
- virt_energy: float32 [30720], replicated, may hold values from 0.5 to 4
- occ_energy: float32 [16], P('groups'), parts along dimension 0, may hold values from -1.5 to -0.3
- domain: int32 [16, 4], P('groups'), parts along dimension 0, may hold values from 0 to 239
- partners: int32 [16, 2], P('groups'), parts along dimension 0, may hold values from 0 to 7, all different within a row
- pair_count: int32 [16], P('groups'), parts along dimension 0, may hold values from 1 to 2, 10 in all
Outputs:
- gamma: bfloat16 [2496, 16, 512], P(('aux', 'occ'), 'groups', 'vir'), parts along dimension 1
There are 2 independent parts, one for each index of `groups`. A program takes and returns all parts, laid end to end along the dimension named above; an argument that names none is the same for every part. Nothing has to cross between parts.
Inputs may be any that keep to these rules, and one draw needn't show every extreme that they name: Each row names 2 different partners; every orbital is some orbital's partner. `pair_count`: some orbital has all 2 slots live.
All inputs are finite; a program needn't handle non-finite values.
Results may differ from a plain program's by a relative error of at most 0.005.
Values may be sent and summed in bfloat16 or wider, within the bound.
A program may use at most 128 MiB of HBM per device.

v0:
```python
import jax
import jax.numpy as jnp
from jax import lax
from jax.sharding import PartitionSpec as P

VB = 128


def select_rows(table, indices, count):
    onehot = (indices[..., None] == jnp.arange(count, dtype=jnp.int32)).astype(jnp.float32)
    return jnp.einsum("...k,kd->...d", onehot, table, precision=lax.Precision.HIGHEST)


def on_device(integrals, virt_energy, occ_energy, domain, partners, pair_count):
    aux_count = lax.axis_size("aux")
    vir_count = lax.axis_size("vir")
    aux_place = lax.axis_index("aux")
    vir_place = lax.axis_index("vir")
    aux_rows, nocc_all, half_width = integrals.shape
    occ_own = nocc_all // aux_count
    slot_count = partners.shape[1]
    block_count = virt_energy.shape[0] // VB
    first_own = aux_place * occ_own
    picked = jnp.take(integrals, partners.reshape(-1), axis=1)
    picked = picked.reshape(aux_rows, aux_count, occ_own * slot_count, half_width)
    own_rows = integrals.reshape(aux_rows, aux_count, occ_own, half_width)
    arrived, own_arrived = (
        lax.all_to_all(picked, "aux", split_axis=1, concat_axis=0, tiled=True),
        lax.all_to_all(own_rows, "aux", split_axis=1, concat_axis=0, tiled=True),
    )
    partner_full = lax.all_gather(arrived, "vir", axis=3, tiled=True)
    own_arrived = own_arrived.reshape(aux_count * aux_rows, occ_own, half_width)
    domain_width = vir_count * half_width
    pair_partial = jnp.einsum(
        "rjsa,rjb->jsab", partner_full, own_arrived, preferred_element_type=jnp.float32
    )
    energy_table = virt_energy.reshape(block_count, VB)
    eps_dom = select_rows(energy_table, domain, block_count).reshape(nocc_all, domain_width)
    own_partners = lax.dynamic_slice_in_dim(partners, first_own, occ_own, 0)
    eps_partner = select_rows(eps_dom, own_partners, nocc_all)
    eps_own = lax.dynamic_slice(eps_dom, (first_own, vir_place * half_width), (occ_own, half_width))
    occ_partner = select_rows(occ_energy[:, None], own_partners, nocc_all)[..., 0]
    occ_own_energy = lax.dynamic_slice_in_dim(occ_energy, first_own, occ_own, 0)
    own_count = lax.dynamic_slice_in_dim(pair_count, first_own, occ_own, 0)
    live_slot = (jnp.arange(slot_count, dtype=jnp.int32)[None, :] < own_count[:, None]).astype(
        jnp.float32
    )
    denominator = (
        eps_partner[:, :, :, None]
        + eps_own[:, None, None, :]
        - occ_partner[:, :, None, None]
        - occ_own_energy[:, None, None, None]
    )
    pair_sums = lax.psum(pair_partial, "occ")
    amplitude = (-(pair_sums / denominator) * live_slot[:, :, None, None]).astype(jnp.bfloat16)
    gamma_rows = jnp.einsum(
        "rjsa,jsab->rjb", partner_full, amplitude, preferred_element_type=jnp.float32
    ).astype(jnp.bfloat16)
    return lax.all_to_all(gamma_rows, "aux", split_axis=0, concat_axis=1, tiled=True)


def solution(mesh):
    in_specs = (
        P(("aux", "occ"), "groups", "vir"),
        P(),
        P("groups"),
        P("groups", None),
        P("groups", None),
        P("groups"),
    )
    out_specs = P(("aux", "occ"), "groups", "vir")
    return jax.shard_map(
        on_device, mesh=mesh, in_specs=in_specs, out_specs=out_specs, check_vma=False
    )
```

profile of v0, /device:TPU:0, one launch (start us, length us, event | category | flops | bytes accessed | tf_op | source)
XLA Modules:
  0.0 185.1 jit_solution(8182170862273645428)
XLA Ops:
  6.5 0.0 copy-start
  6.5 0.0 all-gather.2.cloned.1.call-start
  6.5 0.8 copy.22
  7.3 0.7 compare_and_fusion
  8.0 0.1 reshape.171
  8.1 7.2 %gather_fusion = bf16[16,312,256]{2,0,1:T(8,128)(2,1)S(1)} fusion(bf16[312,8,256]{2,1,0:T(8,128)(2,1)} %param.6, s32[1024]{0:T(1024)S(1)} %pad_clamp_fusion), kind=kCustom, calls=%fused_computation | custom fusion | bytes 5111872 | tf_op jit(solution)/shard_map/jit(_take)/gather | solution.py:24
  15.3 2.4 %copy.28 = bf16[312,16,256]{2,0,1:T(8,128)(2,1)} copy(bf16[312,16,256]{2,1,0:T(8,128)(2,1)S(1)} %bitcast.74) | data formatting | bytes 5111808 | tf_op jit(solution)/shard_map/jit(_take)/gather | solution.py:24
  17.7 0.1 copy.21
  17.7 2.0 %broadcast_select_fusion = bf16[312,8,2,256]{3,0,2,1:T(8,128)(2,1)S(1)} fusion(bf16[312,8,2,256]{3,0,2,1:T(8,128)(2,1)} %bitcast.76, pred[8,2]{1,0:T(8,128)(4,1)S(1)} %copy.21), kind=kLoop, calls=%fused_computation.8 | loop fusion | flops 1277952 | bytes 5111824 | tf_op jit(solution)/shard_map/jit(_take)/select_n | solution.py:24
  19.8 65.2 %all_to_all.51 = bf16[312,8,2,256]{3,0,2,1:T(8,128)(2,1)S(1)} all-to-all(bf16[312,8,2,256]{3,0,2,1:T(8,128)(2,1)S(1)} %broadcast_select_fusion), channel_id=1, replica_groups=mesh['groups'=2,'aux'=8,'occ'=1,'vir'=2] {'aux'}, dimensions={1} | all-to-all | bytes 5111808 | tf_op jit(solution)/shard_map/all_to_all | solution.py:28
  85.0 1.7 copy.24
  86.7 0.0 copy-start.1
  86.7 0.0 all-gather.2.cloned.1.call-update
  86.7 1.3 copy-done.1
  88.0 0.0 copy-start.2
  88.0 0.0 copy-start.4
  88.0 0.0 copy-start.5
  88.0 0.0 copy-start.3
  88.0 1.3 copy.31
  89.3 3.6 %all-to-all-start.1 = ((bf16[312,8,1,256]{3,0,2,1:T(8,128)(2,1)}), bf16[312,8,1,256]{3,0,2,1:T(8,128)(2,1)S(1)}, u32[]{:S(2)}, u32[]{:S(2)}) async-start(bf16[312,8,1,256]{3,0,2,1:T(8,128)(2,1)} %bitcast.73), calls=%async_computation.1 | async-start | bytes 2555904 | tf_op jit(solution)/shard_map/all_to_all | solution.py:29
  92.9 0.0 copy-done.2
  92.9 0.2 dynamic-slice_reduce_fusion
  93.1 0.0 copy-done.4
  93.1 0.7 dynamic_slice.18
  93.8 0.0 copy-done.5
  93.8 0.6 dynamic_slice.17
  94.4 0.0 copy-done
  94.4 0.0 copy-done.3
  94.4 0.2 convolution_bitcast_fusion
  94.6 0.1 dynamic_slice.16
  94.7 0.6 compare_convert_fusion
  95.3 0.2 convolution_bitcast_fusion.1
  95.5 0.2 fusion.34
  95.7 27.5 %all-to-all-done.1 = bf16[312,8,1,256]{3,0,2,1:T(8,128)(2,1)S(1)} async-done(((bf16[312,8,1,256]{3,0,2,1:T(8,128)(2,1)}), bf16[312,8,1,256]{3,0,2,1:T(8,128)(2,1)S(1)}, u32[]{:S(2)}, u32[]{:S(2)}) %all-to-all-start.1) | async-done | bytes 1277984 | tf_op jit(solution)/shard_map/all_to_all | solution.py:29
  123.2 0.0 all-gather.2.cloned.1.call-done
  123.2 11.2 %fusion.10 = bf16[2496,1,256]{2,0,1:T(8,128)(2,1)} fusion(bf16[2496,1,2,512]{3,0,2,1:T(8,128)(2,1)} %all-gather.2.cloned.1.call-done, bf16[2496,256,1]{1,0,2:T(8,128)(2,1)S(1)} %bitcast.79, f32[2]{0:T(128)S(1)} %compare_convert_fusion, f32[]{:T(128)} %bitcast.19, f32[2]{0:T(128)S(1)} %convolution_bitcast_fusion.1, f32[256]{0:T(256)S(1)} %bitcast.80, ...), kind=kOutput, calls=%fused_computation.7 | convolution fusion | flops 2619719680 | bytes 7672852 | tf_op jit(solution)/shard_map/rjsa,jsab->rjb/dot_general | solution.py:56
  134.4 0.5 broadcast.96
  134.9 2.9 %reduce.2 = bf16[2496,256]{1,0:T(8,128)(2,1)S(1)} reduce(bf16[2496,1,256]{2,0,1:T(8,128)(2,1)} %fusion.10, bf16[]{:T(256)} %broadcast.96), dimensions={1}, to_apply=%copy.26.reduce_sub_computation | reduce | bytes 2555906 | tf_op jit(solution)/shard_map/convert_element_type | solution.py:58
  137.7 0.3 reshape.191
  138.1 34.3 %all_to_all.52 = bf16[8,2,39936]{2,1,0:T(2,128)(2,1)} all-to-all(bf16[8,2,39936]{2,1,0:T(2,128)(2,1)S(1)} %reshape.191), channel_id=1, replica_groups=mesh['groups'=2,'aux'=8,'occ'=1,'vir'=2] {'aux'}, dimensions={0} | all-to-all | bytes 2555904 | tf_op jit(solution)/shard_map/all_to_all | solution.py:59
  172.4 4.3 %reshape.192 = bf16[2496,1,256]{2,1,0:T(2,128)(2,1)S(1)} reshape(bf16[8,2,39936]{2,1,0:T(2,128)(2,1)} %all_to_all.52) | data formatting | bytes 2555904
  176.7 0.3 copy.29
  177.0 1.3 copy.27
  (2 shorter events, 0.0 us)
Async XLA Ops:
  6.5 87.8 %copy-start = (f32[30720]{0:T(1024)S(1)}, f32[30720]{0:T(1024)}, u32[]{:S(2)}) copy-start(f32[30720]{0:T(1024)} %param.7) | copy-start | bytes 368644
  6.5 116.7 %all-gather.2.cloned.1.call-start = ((), (), s32[]{:S(2)}) async-start(), calls=%async_computation.3 | async-start | bytes 7667712 | tf_op jit(solution)/shard_map/all_gather | solution.py:31
  86.7 1.3 copy-start.1
  88.0 4.9 %copy-start.2 = (s32[8,2]{0,1:T(2,128)S(1)}, s32[8,2]{0,1:T(2,128)}, u32[]{:S(2)}) copy-start(s32[8,2]{0,1:T(2,128)} %param.10) | copy-start | bytes 196
  88.0 5.1 %copy-start.4 = (s32[8]{0:T(128)S(1)}, s32[8]{0:T(128)}, u32[]{:S(2)}) copy-start(s32[8]{0:T(128)} %param.11) | copy-start | bytes 100
  88.0 5.8 %copy-start.5 = (f32[8]{0:T(128)S(1)}, f32[8]{0:T(128)}, u32[]{:S(2)}) copy-start(f32[8]{0:T(128)} %param.8) | copy-start | bytes 100
  88.0 6.4 %copy-start.3 = (s32[8,4]{0,1:T(4,128)S(1)}, s32[8,4]{0,1:T(4,128)}, u32[]{:S(2)}) copy-start(s32[8,4]{0,1:T(4,128)} %param.9) | copy-start | bytes 388
  89.3 33.9 %all-to-all-start.1 = ((bf16[312,8,1,256]{3,0,2,1:T(8,128)(2,1)}), bf16[312,8,1,256]{3,0,2,1:T(8,128)(2,1)S(1)}, u32[]{:S(2)}, u32[]{:S(2)}) async-start(bf16[312,8,1,256]{3,0,2,1:T(8,128)(2,1)} %bitcast.73), calls=%async_computation.1 | async-start | bytes 2555904 | tf_op jit(solution)/shard_map/all_to_all | solution.py:29
Sparse Core Ops, SparseCore 0:
  86.8 12.9 all-gather.1
where the time goes:
time: 186 us; the launch traced here: 185 us
  blocking collectives  99.5 us (53%)
  waiting for transfers between devices  27.5 us (15%)
  local copies, waits for them, and re-layouts  23 us (12%)
  between operations  13.5 us (7%)
  matrix products  11.7 us (6%)
  other arithmetic  6.21 us (3%)
  starting transfers between devices  3.6 us (2%)
    all_to_all x1, blocking collectives, on_device(): lax.all_to_all(picked, 'aux', split_axis=1, concat_axis=0, tiled=True)  65.2 us
    all_to_all x1, blocking collectives, on_device(): lax.all_to_all(gamma_rows, 'aux', split_axis=0, concat_axis=1, tiled=True)  34.3 us
    all_to_all x1, waiting for transfers between devices, on_device(): lax.all_to_all(own_rows, 'aux', split_axis=1, concat_axis=0, tiled=True)  27.5 us
    dot_general x1, matrix products, on_device(): jnp.einsum('rjsa,jsab->rjb', partner_full, amplitude, preferred_element_t...  11.2 us
    gather x2, local copies, waits for them, and re-layouts, on_device(): picked = jnp.take(integrals, partners.reshape(-1), axis=1)  9.54 us
    unnamed x17, local copies, waits for them, and re-layouts  8.32 us
  transfers between devices with their start and end apart: 2, of which 1 were waited for; matrix products, arithmetic and copies ran while one was open for 2% of the time, Pallas kernels for 0%

commit v1 on v0

v1 whole, which is shorter than its diff:
```python
import functools
import math

import jax
import jax.numpy as jnp
from jax import lax
from jax.experimental import pallas as pl
from jax.experimental.pallas import tpu as pltpu
from jax.sharding import PartitionSpec as P

VB = 128
MESH = pl.DeviceIdType.MESH
BF16 = jnp.bfloat16
F32 = jnp.float32


def grid_of(aux_count, occ_count):
    if occ_count == 1:
        return aux_count // 2, 2
    return aux_count, occ_count


def ring_place(z, x, Z, X):
    comb = x * (Z - 1) + jnp.where(x % 2 == 0, z - 1, Z - 1 - z)
    return jnp.where(z == 0, X * (Z - 1) + X - 1 - x, comb)


def ring_point(p, Z, X):
    x = p // (Z - 1)
    r = p % (Z - 1)
    comb_z = jnp.where(x % 2 == 0, r + 1, Z - 1 - r)
    back = p >= X * (Z - 1)
    return jnp.where(back, 0, comb_z), jnp.where(back, X - 1 - (p - X * (Z - 1)), x)


def steps(low, high, body):
    if high - low <= 6:
        for t in range(low, high):
            body(t)
    elif high > low:
        lax.fori_loop(low, high, lambda t, c: (body(t), c)[1], 0)


def kernel(
    aux_count, occ_count, pair_total,
    partners, domain, count, occ_energy, virt, own,
    out,
    peer, sums, amp, sent, came, turned, second,
    peer_sem, rs_send, rs_recv, ag_send, ag_recv,
):
    nocc, aux_rows, half_width = own.shape
    width = 2 * half_width
    Z, X = grid_of(aux_count, occ_count)
    N = Z * X
    H = N // 2
    rows = pair_total * width // N
    sub_rows = (-(-rows // 32) * 16, rows - (-(-rows // 32) * 16))
    sub_off = (0, sub_rows[0])
    group, aux, occ, v = (lax.axis_index(a) for a in ("groups", "aux", "occ", "vir"))
    if occ_count == 1:
        z, x = aux // X, aux % X
    else:
        z, x = aux, occ
    p = ring_place(z, x, Z, X)

    def device(q):
        qz, qx = ring_point(lax.rem(q + N, N), Z, X)
        if occ_count == 1:
            return (group, qz * X + qx, 0, v)
        return (group, qz, qx, v)

    target = (device(p + 1), device(p - 1))
    other = (group, aux, occ, 1 - v)
    barrier = pltpu.get_barrier_semaphore()
    for d in (*target, other):
        pl.semaphore_signal(barrier, inc=1, device_id=d, device_id_type=MESH)
    pl.semaphore_wait(barrier, 3)

    swap = pltpu.make_async_remote_copy(
        src_ref=own, dst_ref=peer, send_sem=peer_sem.at[0], recv_sem=peer_sem.at[1],
        device_id=other, device_id_type=MESH,
    )
    swap.start()

    ahead = []
    running = jnp.int32(0)
    for j in range(nocc):
        ahead.append(running)
        running = running + count[j] - 1
    def holds(j, e):
        apart = ahead[j] - e
        return (count[j] - 1) * jnp.maximum(1 - jnp.maximum(apart, -apart), 0)

    extras = pair_total - nocc
    pair_j = [jnp.int32(j) for j in range(nocc)]
    pair_i = [partners[j, 0] for j in range(nocc)]
    for e in range(extras):
        pair_j.append(sum(holds(j, e) * j for j in range(nocc)))
        pair_i.append(sum(holds(j, e) * partners[j, 1] for j in range(nocc)))

    def mul_t(a, b):
        return lax.dot_general(a, b, (((0,), (0,)), ((), ())), preferred_element_type=F32)

    for k in range(pair_total):
        at = pl.multiple_of(k * width + v * half_width, half_width)
        sums[pl.ds(at, half_width), :] = mul_t(own[pair_i[k]], own[pair_j[k]])
    swap.wait()
    for k in range(pair_total):
        at = pl.multiple_of(k * width + (1 - v) * half_width, half_width)
        sums[pl.ds(at, half_width), :] = mul_t(peer[pair_i[k]], own[pair_j[k]])

    def chunk_rows(c, sub):
        c = lax.rem(c + 2 * N, N)
        return pl.ds(pl.multiple_of(c * rows + sub_off[sub], 16), sub_rows[sub])

    def part(sub):
        return pl.ds(sub_off[sub], sub_rows[sub])

    def rs_copy(d, t, sub):
        return pltpu.make_async_remote_copy(
            src_ref=sent.at[d, t, part(sub), :], dst_ref=came.at[d, t, part(sub), :],
            send_sem=rs_send.at[d, t, sub], recv_sem=rs_recv.at[d, t, sub],
            device_id=target[d], device_id_type=MESH,
        )

    def rs_step(d, t, sub, add):
        sign = 1 - 2 * d
        value = sums[chunk_rows(p + sign * (H - t), sub), :]
        if add:
            rs_copy(d, t - 1, sub).wait_recv()
            value = value + came[d, t - 1, part(sub), :].astype(F32)
        sent[d, t, part(sub), :] = value.astype(BF16)
        rs_copy(d, t, sub).start()

    rs_step(0, 0, 0, False)
    rs_step(1, 0, 1, False)
    rs_step(0, 1, 1, False)
    rs_step(1, 1, 0, False)
    rs_step(0, 1, 0, True)
    rs_step(1, 1, 1, True)

    def rs_body(t):
        rs_step(0, t, 1, True)
        rs_step(1, t, 0, True)
        rs_step(0, t, 0, True)
        rs_step(1, t, 1, True)

    steps(2, H, rs_body)

    def ag_copy(d, t, sub):
        where = chunk_rows(p - (1 - 2 * d) * t, sub)
        return pltpu.make_async_remote_copy(
            src_ref=amp.at[where, :], dst_ref=amp.at[where, :],
            send_sem=ag_send.at[d, t, sub], recv_sem=ag_recv.at[d, t, sub],
            device_id=target[d], device_id_type=MESH,
        )

    piece = math.gcd(math.gcd(sub_rows[0], sub_rows[1]), VB)
    blocks = half_width // VB

    def amplitude(sub):
        rs_copy(0, H - 1, sub).wait_recv()
        rs_copy(1, H - 1, sub).wait_recv()
        for q in range(sub_rows[sub] // piece):
            local = sub_off[sub] + q * piece
            row = pl.multiple_of(p * rows + local, piece)
            k = row // width
            a = row % width
            j = jnp.int32(0)
            i = jnp.int32(0)
            for m in range(pair_total):
                same = (k == m).astype(jnp.int32)
                j = j + same * pair_j[m]
                i = i + same * pair_i[m]
            eps_a = virt[domain[i, a // VB]]
            turned[...] = jnp.broadcast_to(eps_a, (VB, VB)).T
            offset = pl.multiple_of(row % VB, piece)
            column = turned[pl.ds(offset, piece), :]
            for h in range(blocks):
                lanes = slice(h * VB, (h + 1) * VB)
                eps_b = virt[domain[j, v * blocks + h]]
                denominator = (column + eps_b) - occ_energy[i] - occ_energy[j]
                total = (
                    sums[pl.ds(row, piece), lanes]
                    + came[0, H - 1, pl.ds(local, piece), lanes].astype(F32)
                    + came[1, H - 1, pl.ds(local, piece), lanes].astype(F32)
                )
                amp[pl.ds(row, piece), lanes] = (-(total / denominator)).astype(BF16)

    for sub in (1, 0):
        amplitude(sub)
        ag_copy(0, 0, sub).start()
        ag_copy(1, 0, sub).start()

    def ag_body(t):
        for sub in (1, 0):
            for d in (0, 1):
                ag_copy(d, t - 1, sub).wait_recv()
                ag_copy(d, t, sub).start()

    steps(1, H - 1, ag_body)
    for d, sub in ((1, 1), (0, 0)):
        ag_copy(d, H - 2, sub).wait_recv()
        ag_copy(d, H - 1, sub).start()
    ag_copy(0, H - 2, 1).wait_recv()
    ag_copy(1, H - 2, 0).wait_recv()
    ag_copy(0, H - 1, 0).wait_recv()
    ag_copy(1, H - 1, 1).wait_recv()

    def mul(a, b):
        return jnp.dot(a, b, preferred_element_type=F32)

    def half_of(k, side):
        return amp[pl.ds(pl.multiple_of(k * width + side * half_width, half_width), half_width), :]

    def pair_product(k):
        i = pair_i[k]
        return mul(own[i], half_of(k, v)) + mul(peer[i], half_of(k, 1 - v))

    for e in range(extras):
        second[e] = pair_product(nocc + e)
    for j in range(nocc):
        value = pair_product(j)
        for e in range(extras):
            value = value + second[e] * holds(j, e).astype(F32)
        out[j] = value.astype(BF16)

    rs_copy(0, 0, 0).wait_send()
    rs_copy(1, 0, 1).wait_send()

    def rs_end(t):
        for d in (0, 1):
            for sub in (0, 1):
                rs_copy(d, t, sub).wait_send()

    steps(1, H, rs_end)

    def ag_end(t):
        for d in (0, 1):
            for sub in (0, 1):
                ag_copy(d, t, sub).wait_send()

    steps(0, H - 1, ag_end)
    ag_copy(0, H - 1, 0).wait_send()
    ag_copy(1, H - 1, 1).wait_send()


def on_device(integrals, virt_energy, occ_energy, domain, partners, pair_count):
    aux_count = lax.axis_size("aux")
    occ_count = lax.axis_size("occ")
    aux_rows, nocc, half_width = integrals.shape
    slot_count = partners.shape[1]
    pair_total = nocc * slot_count * 5 // 8
    width = half_width * lax.axis_size("vir")
    N = aux_count * occ_count
    H = N // 2
    rows = pair_total * width // N
    smem = pl.BlockSpec(memory_space=pltpu.SMEM)
    vmem = pl.BlockSpec(memory_space=pltpu.VMEM)
    gamma = pl.pallas_call(
        functools.partial(kernel, aux_count, occ_count, pair_total),
        out_shape=jax.ShapeDtypeStruct((nocc, aux_rows, half_width), BF16),
        in_specs=[smem] * 4 + [vmem] * 2,
        out_specs=vmem,
        scratch_shapes=[
            pltpu.VMEM((nocc, aux_rows, half_width), BF16),
            pltpu.VMEM((pair_total * width, half_width), F32),
            pltpu.VMEM((pair_total * width, half_width), BF16),
            pltpu.VMEM((2, H, rows, half_width), BF16),
            pltpu.VMEM((2, H, rows, half_width), BF16),
            pltpu.VMEM((VB, VB), F32),
            pltpu.VMEM((pair_total - nocc, aux_rows, half_width), F32),
            pltpu.SemaphoreType.DMA((2,)),
            pltpu.SemaphoreType.DMA((2, H, 2)),
            pltpu.SemaphoreType.DMA((2, H, 2)),
            pltpu.SemaphoreType.DMA((2, H, 2)),
            pltpu.SemaphoreType.DMA((2, H, 2)),
        ],
        compiler_params=pltpu.CompilerParams(
            collective_id=0, has_side_effects=True, vmem_limit_bytes=56 * 1024 * 1024
        ),
    )(
        partners, domain, pair_count, occ_energy,
        virt_energy.reshape(-1, 1, VB), jnp.transpose(integrals, (1, 0, 2)),
    )
    return jnp.transpose(gamma, (1, 0, 2))


def solution(mesh):
    in_specs = (
        P(("aux", "occ"), "groups", "vir"),
        P(),
        P("groups"),
        P("groups", None),
        P("groups", None),
        P("groups"),
    )
    out_specs = P(("aux", "occ"), "groups", "vir")
    return jax.shard_map(
        on_device, mesh=mesh, in_specs=in_specs, out_specs=out_specs, check_vma=False
    )
```

time: 186 us -> 73.9 us (0.40)
  blocking collectives: 99.5 us -> 0 us
  Pallas kernels: 0 us -> 65.7 us
  waiting for transfers between devices: 27.5 us -> 0 us
  local copies, waits for them, and re-layouts: 23 us -> 7.9 us
  between operations: 13.5 us -> 0.01 us
  matrix products: 11.7 us -> 0 us
  other arithmetic: 6.21 us -> 0 us
  starting transfers between devices: 3.6 us -> 0 us
    all_to_all x2 -> x0, blocking collectives: 99.5 us -> none  [the longest x1 65.2 us: on_device(): lax.all_to_all(picked, 'aux', split_axis=1, concat_axis=0, tiled=True)]
    pallas_call x0 -> x1, Pallas kernels: none -> 65.7 us  [on_device(): pl.pallas_call(functools.partial(kernel, aux_count, occ_count, pair_total...]
    all_to_all x1 -> x0, waiting for transfers between devices: 27.5 us -> none  [on_device(): lax.all_to_all(own_rows, 'aux', split_axis=1, concat_axis=0, tiled=True)]
    dot_general x4 -> x0, matrix products: 11.7 us -> none  [the longest x1 11.2 us: on_device(): jnp.einsum('rjsa,jsab->rjb', partner_full, amplitude, preferred_element_t...]
    gather x2 -> x0, local copies, waits for them, and re-layouts: 9.54 us -> none  [on_device(): picked = jnp.take(integrals, partners.reshape(-1), axis=1)]
    all_to_all x1 -> x0, starting transfers between devices: 3.6 us -> none  [on_device(): lax.all_to_all(own_rows, 'aux', split_axis=1, concat_axis=0, tiled=True)]
    convert_element_type x2 -> x0, other arithmetic: 3.49 us -> none  [the longest x1 2.85 us: on_device(): gamma_rows = jnp.einsum('rjsa,jsab->rjb', partner_full, amplitude, prefer...]
    unnamed x17 -> x3, local copies, waits for them, and re-layouts: 8.32 us -> 5.29 us
  transfers between devices with their start and end apart: 2 -> 0, of which waited for: 1 -> 0; matrix products, arithmetic and copies ran while one was open for 2% -> 0% of each run, Pallas kernels for 0% -> 0%
where the time goes in v1:
time: 73.9 us; the launch traced here: 73.6 us
  Pallas kernels  65.7 us (89%)
  local copies, waits for them, and re-layouts  7.9 us (11%)
    pallas_call x1, Pallas kernels, on_device(): pl.pallas_call(functools.partial(kernel, aux_count, occ_count, pair_total...  65.7 us
    unnamed x3, local copies, waits for them, and re-layouts  5.29 us
    transpose x1, local copies, waits for them, and re-layouts, on_device(): return jnp.transpose(gamma, (1, 0, 2))  2.61 us

profile of v1, /device:TPU:0, one launch (start us, length us, event | category | flops | bytes accessed | tf_op | source)
XLA Modules:
  0.0 73.6 jit_solution(80533677165925753)
XLA Ops:
  0.0 1.3 %copy.9.domain = s32[8,4]{1,0:T(8,128)} copy(s32[8,4]{0,1:T(4,128)} %param.9) | data formatting | bytes 256 | tf_op args[3]
  1.3 1.3 %copy.8.partners = s32[8,2]{1,0:T(8,128)} copy(s32[8,2]{0,1:T(2,128)} %param.10) | data formatting | bytes 128 | tf_op args[4]
  2.7 2.6 %copy.12 = bf16[312,8,256]{2,0,1:T(8,128)(2,1)} copy(bf16[312,8,256]{2,1,0:T(8,128)(2,1)} %param.6) | data formatting | bytes 2555904 | tf_op args[0]
  5.3 65.7 %shard_map.64 = bf16[8,312,256]{2,1,0:T(8,128)(2,1)} custom-call(s32[8,2]{1,0:T(8,128)} %copy.8.partners, s32[8,4]{1,0:T(8,128)} %copy.9.domain, s32[8]{0:T(128)} %count.1, f32[8]{0:T(128)} %occ_energy.1, f32[240,1,128]{2,1,0:T(1,128)} %bitcast.7, bf16[8,312,256]{2,1,0:T(8,128)(2,1)} %bitcast.6), custom_call_target="tpu_custom_call" | custom-call | tf_op jit(solution)/shard_map/pallas_call | solution.py:260
  71.0 2.6 %copy.10 = bf16[312,8,256]{2,1,0:T(8,128)(2,1)} copy(bf16[312,8,256]{2,0,1:T(8,128)(2,1)} %bitcast.5) | data formatting | bytes 2555904 | tf_op jit(solution)/shard_map/transpose | solution.py:286

commit v2 on v1

--- a/solution.py
+++ b/solution.py
@@ -33,6 +33,19 @@
     return jnp.where(back, 0, comb_z), jnp.where(back, X - 1 - (p - X * (Z - 1)), x)
 
 
+SUBS = 4
+FIRST = ((0, 1), (2, 3))
+RS_ORDER = ((2, 3, 0, 1), (0, 1, 2, 3))
+AG_ORDER = (0, 2, 1, 3)
+
+
+def cut(rows):
+    units = rows // 16
+    ends = [-(-units * (n + 1) // SUBS) * 16 for n in range(SUBS)]
+    starts = [0] + ends[:-1]
+    return tuple(e - b for b, e in zip(starts, ends)), tuple(starts)
+
+
 def steps(low, high, body):
     if high - low <= 6:
         for t in range(low, high):
@@ -45,7 +58,7 @@
     aux_count, occ_count, pair_total,
     partners, domain, count, occ_energy, virt, own,
     out,
-    peer, sums, amp, sent, came, turned, second,
+    peer, sums, amp, sent, came, turned, scale, second,
     peer_sem, rs_send, rs_recv, ag_send, ag_recv,
 ):
     nocc, aux_rows, half_width = own.shape
@@ -54,8 +67,7 @@
     N = Z * X
     H = N // 2
     rows = pair_total * width // N
-    sub_rows = (-(-rows // 32) * 16, rows - (-(-rows // 32) * 16))
-    sub_off = (0, sub_rows[0])
+    sub_rows, sub_off = cut(rows)
     group, aux, occ, v = (lax.axis_index(a) for a in ("groups", "aux", "occ", "vir"))
     if occ_count == 1:
         z, x = aux // X, aux % X
@@ -93,10 +105,10 @@
 
     extras = pair_total - nocc
     pair_j = [jnp.int32(j) for j in range(nocc)]
-    pair_i = [partners[j, 0] for j in range(nocc)]
+    pair_i = [partners[0, j] for j in range(nocc)]
     for e in range(extras):
         pair_j.append(sum(holds(j, e) * j for j in range(nocc)))
-        pair_i.append(sum(holds(j, e) * partners[j, 1] for j in range(nocc)))
+        pair_i.append(sum(holds(j, e) * partners[1, j] for j in range(nocc)))
 
     def mul_t(a, b):
         return lax.dot_general(a, b, (((0,), (0,)), ((), ())), preferred_element_type=F32)
@@ -132,18 +144,41 @@
         sent[d, t, part(sub), :] = value.astype(BF16)
         rs_copy(d, t, sub).start()
 
-    rs_step(0, 0, 0, False)
-    rs_step(1, 0, 1, False)
-    rs_step(0, 1, 1, False)
-    rs_step(1, 1, 0, False)
-    rs_step(0, 1, 0, True)
-    rs_step(1, 1, 1, True)
+    for n in range(SUBS // 2):
+        for d in (0, 1):
+            rs_step(d, 0, FIRST[d][n], False)
+    for n in range(SUBS // 2):
+        for d in (0, 1):
+            rs_step(d, 1, RS_ORDER[d][n], False)
+
+    piece = math.gcd(rows, VB)
+    blocks = half_width // VB
+    for q in range(rows // piece):
+        row = pl.multiple_of(p * rows + q * piece, piece)
+        k = row // width
+        a = row % width
+        j = jnp.int32(0)
+        i = jnp.int32(0)
+        for m in range(pair_total):
+            same = (k == m).astype(jnp.int32)
+            j = j + same * pair_j[m]
+            i = i + same * pair_i[m]
+        eps_a = virt[domain[a // VB, i]]
+        turned[...] = jnp.broadcast_to(eps_a, (VB, VB)).T
+        column = turned[pl.ds(pl.multiple_of(row % VB, piece), piece), :]
+        for h in range(blocks):
+            eps_b = virt[domain[v * blocks + h, j]]
+            denominator = (column + eps_b) - occ_energy[i] - occ_energy[j]
+            scale[pl.ds(q * piece, piece), slice(h * VB, (h + 1) * VB)] = -1.0 / denominator
+
+    for n in range(SUBS // 2, SUBS):
+        for d in (0, 1):
+            rs_step(d, 1, RS_ORDER[d][n], True)
 
     def rs_body(t):
-        rs_step(0, t, 1, True)
-        rs_step(1, t, 0, True)
-        rs_step(0, t, 0, True)
-        rs_step(1, t, 1, True)
+        for n in range(SUBS):
+            for d in (0, 1):
+                rs_step(d, t, RS_ORDER[d][n], True)
 
     steps(2, H, rs_body)
 
@@ -155,57 +190,33 @@
             device_id=target[d], device_id_type=MESH,
         )
 
-    piece = math.gcd(math.gcd(sub_rows[0], sub_rows[1]), VB)
-    blocks = half_width // VB
-
-    def amplitude(sub):
-        rs_copy(0, H - 1, sub).wait_recv()
-        rs_copy(1, H - 1, sub).wait_recv()
-        for q in range(sub_rows[sub] // piece):
-            local = sub_off[sub] + q * piece
-            row = pl.multiple_of(p * rows + local, piece)
-            k = row // width
-            a = row % width
-            j = jnp.int32(0)
-            i = jnp.int32(0)
-            for m in range(pair_total):
-                same = (k == m).astype(jnp.int32)
-                j = j + same * pair_j[m]
-                i = i + same * pair_i[m]
-            eps_a = virt[domain[i, a // VB]]
-            turned[...] = jnp.broadcast_to(eps_a, (VB, VB)).T
-            offset = pl.multiple_of(row % VB, piece)
-            column = turned[pl.ds(offset, piece), :]
-            for h in range(blocks):
-                lanes = slice(h * VB, (h + 1) * VB)
-                eps_b = virt[domain[j, v * blocks + h]]
-                denominator = (column + eps_b) - occ_energy[i] - occ_energy[j]
-                total = (
-                    sums[pl.ds(row, piece), lanes]
-                    + came[0, H - 1, pl.ds(local, piece), lanes].astype(F32)
-                    + came[1, H - 1, pl.ds(local, piece), lanes].astype(F32)
-                )
-                amp[pl.ds(row, piece), lanes] = (-(total / denominator)).astype(BF16)
-
-    for sub in (1, 0):
-        amplitude(sub)
-        ag_copy(0, 0, sub).start()
-        ag_copy(1, 0, sub).start()
+    for sub in AG_ORDER:
+        for d in (0, 1):
+            rs_copy(d, H - 1, sub).wait_recv()
+        total = (
+            sums[chunk_rows(p, sub), :]
+            + came[0, H - 1, part(sub), :].astype(F32)
+            + came[1, H - 1, part(sub), :].astype(F32)
+        )
+        amp[chunk_rows(p, sub), :] = (total * scale[part(sub), :]).astype(BF16)
+        for d in (0, 1):
+            ag_copy(d, 0, sub).start()
 
     def ag_body(t):
-        for sub in (1, 0):
+        for sub in AG_ORDER:
             for d in (0, 1):
                 ag_copy(d, t - 1, sub).wait_recv()
                 ag_copy(d, t, sub).start()
 
     steps(1, H - 1, ag_body)
-    for d, sub in ((1, 1), (0, 0)):
-        ag_copy(d, H - 2, sub).wait_recv()
-        ag_copy(d, H - 1, sub).start()
-    ag_copy(0, H - 2, 1).wait_recv()
-    ag_copy(1, H - 2, 0).wait_recv()
-    ag_copy(0, H - 1, 0).wait_recv()
-    ag_copy(1, H - 1, 1).wait_recv()
+    for sub in AG_ORDER:
+        for d in (0, 1):
+            ag_copy(d, H - 2, sub).wait_recv()
+            if sub in FIRST[d]:
+                ag_copy(d, H - 1, sub).start()
+    for d in (0, 1):
+        for sub in FIRST[d]:
+            ag_copy(d, H - 1, sub).wait_recv()
 
     def mul(a, b):
         return jnp.dot(a, b, preferred_element_type=F32)
@@ -225,24 +236,18 @@
             value = value + second[e] * holds(j, e).astype(F32)
         out[j] = value.astype(BF16)
 
-    rs_copy(0, 0, 0).wait_send()
-    rs_copy(1, 0, 1).wait_send()
-
-    def rs_end(t):
-        for d in (0, 1):
-            for sub in (0, 1):
-                rs_copy(d, t, sub).wait_send()
-
-    steps(1, H, rs_end)
-
-    def ag_end(t):
-        for d in (0, 1):
-            for sub in (0, 1):
+    for d in (0, 1):
+        for sub in FIRST[d]:
+            rs_copy(d, 0, sub).wait_send()
+            ag_copy(d, H - 1, sub).wait_send()
+
+    def end(t):
+        for d in (0, 1):
+            for sub in range(SUBS):
+                rs_copy(d, t + 1, sub).wait_send()
                 ag_copy(d, t, sub).wait_send()
 
-    steps(0, H - 1, ag_end)
-    ag_copy(0, H - 1, 0).wait_send()
-    ag_copy(1, H - 1, 1).wait_send()
+    steps(0, H - 1, end)
 
 
 def on_device(integrals, virt_energy, occ_energy, domain, partners, pair_count):
@@ -269,18 +274,19 @@
             pltpu.VMEM((2, H, rows, half_width), BF16),
             pltpu.VMEM((2, H, rows, half_width), BF16),
             pltpu.VMEM((VB, VB), F32),
+            pltpu.VMEM((rows, half_width), F32),
             pltpu.VMEM((pair_total - nocc, aux_rows, half_width), F32),
             pltpu.SemaphoreType.DMA((2,)),
-            pltpu.SemaphoreType.DMA((2, H, 2)),
-            pltpu.SemaphoreType.DMA((2, H, 2)),
-            pltpu.SemaphoreType.DMA((2, H, 2)),
-            pltpu.SemaphoreType.DMA((2, H, 2)),
+            pltpu.SemaphoreType.DMA((2, H, SUBS)),
+            pltpu.SemaphoreType.DMA((2, H, SUBS)),
+            pltpu.SemaphoreType.DMA((2, H, SUBS)),
+            pltpu.SemaphoreType.DMA((2, H, SUBS)),
         ],
         compiler_params=pltpu.CompilerParams(
             collective_id=0, has_side_effects=True, vmem_limit_bytes=56 * 1024 * 1024
         ),
     )(
-        partners, domain, pair_count, occ_energy,
+        partners.T, domain.T, pair_count, occ_energy,
         virt_energy.reshape(-1, 1, VB), jnp.transpose(integrals, (1, 0, 2)),
     )
     return jnp.transpose(gamma, (1, 0, 2))

time: 73.9 us -> 69.9 us (0.946)
  local copies, waits for them, and re-layouts: 7.9 us -> 5.21 us
  Pallas kernels: 65.7 us -> 64.5 us
    unnamed x3 -> x1, local copies, waits for them, and re-layouts: 5.29 us -> 2.6 us
    pallas_call x1, Pallas kernels: 65.7 us -> 64.5 us  [on_device(): pl.pallas_call(functools.partial(kernel, aux_count, occ_count, pair_total...]
where the time goes in v2:
time: 69.9 us; the launch traced here: 69.7 us
  Pallas kernels  64.5 us (92%)
  local copies, waits for them, and re-layouts  5.21 us (7%)
    pallas_call x1, Pallas kernels, on_device(): pl.pallas_call(functools.partial(kernel, aux_count, occ_count, pair_total...  64.5 us
    transpose x1, local copies, waits for them, and re-layouts, on_device(): return jnp.transpose(gamma, (1, 0, 2))  2.61 us
    unnamed x1, local copies, waits for them, and re-layouts  2.6 us

profile of v2, /device:TPU:0, one launch (start us, length us, event | category | flops | bytes accessed | tf_op | source)
XLA Modules:
  0.0 69.7 jit_solution(10208339569517716722)
XLA Ops:
  0.0 2.6 %copy.10 = bf16[312,8,256]{2,0,1:T(8,128)(2,1)} copy(bf16[312,8,256]{2,1,0:T(8,128)(2,1)} %param.6) | data formatting | bytes 2555904 | tf_op args[0]
  2.6 64.5 %shard_map.64 = bf16[8,312,256]{2,1,0:T(8,128)(2,1)} custom-call(s32[2,8]{1,0:T(2,128)} %bitcast.11, s32[4,8]{1,0:T(4,128)} %bitcast.10, s32[8]{0:T(128)} %count.1, f32[8]{0:T(128)} %occ_energy.1, f32[240,1,128]{2,1,0:T(1,128)} %bitcast.9, bf16[8,312,256]{2,1,0:T(8,128)(2,1)} %bitcast.8), custom_call_target="tpu_custom_call" | custom-call | tf_op jit(solution)/shard_map/pallas_call | solution.py:265
  67.1 2.6 %copy.8 = bf16[312,8,256]{2,1,0:T(8,128)(2,1)} copy(bf16[312,8,256]{2,0,1:T(8,128)(2,1)} %bitcast.7) | data formatting | bytes 2555904 | tf_op jit(solution)/shard_map/transpose | solution.py:292

commit v3 on v2

--- a/solution.py
+++ b/solution.py
@@ -113,17 +113,32 @@
     def mul_t(a, b):
         return lax.dot_general(a, b, (((0,), (0,)), ((), ())), preferred_element_type=F32)
 
-    for k in range(pair_total):
-        at = pl.multiple_of(k * width + v * half_width, half_width)
-        sums[pl.ds(at, half_width), :] = mul_t(own[pair_i[k]], own[pair_j[k]])
-    swap.wait()
-    for k in range(pair_total):
-        at = pl.multiple_of(k * width + (1 - v) * half_width, half_width)
-        sums[pl.ds(at, half_width), :] = mul_t(peer[pair_i[k]], own[pair_j[k]])
+    split = rows % 64 == 0
+    half_rows = rows // 2
+
+    def half_at(k, far):
+        if split:
+            return pl.ds((far * pair_total + k) * half_width, half_width)
+        side = 1 - v if far else v
+        return pl.ds(pl.multiple_of(k * width + side * half_width, half_width), half_width)
 
     def chunk_rows(c, sub):
         c = lax.rem(c + 2 * N, N)
-        return pl.ds(pl.multiple_of(c * rows + sub_off[sub], 16), sub_rows[sub])
+        if split:
+            far = sub_off[sub] // half_rows
+            start = far * pair_total * half_width + c * half_rows + sub_off[sub] - far * half_rows
+        else:
+            start = c * rows + sub_off[sub]
+        return pl.ds(pl.multiple_of(start, 16), sub_rows[sub])
+
+    def pair_sums(source, far):
+        for k in range(pair_total):
+            sums[half_at(k, far), :] = mul_t(source[pair_i[k]], own[pair_j[k]])
+
+    pair_sums(own, 0)
+    if not split:
+        swap.wait()
+        pair_sums(peer, 1)
 
     def part(sub):
         return pl.ds(sub_off[sub], sub_rows[sub])
@@ -144,19 +159,28 @@
         sent[d, t, part(sub), :] = value.astype(BF16)
         rs_copy(d, t, sub).start()
 
-    for n in range(SUBS // 2):
-        for d in (0, 1):
-            rs_step(d, 0, FIRST[d][n], False)
-    for n in range(SUBS // 2):
-        for d in (0, 1):
-            rs_step(d, 1, RS_ORDER[d][n], False)
-
-    piece = math.gcd(rows, VB)
+    for sub in (0, 1):
+        for d in (0, 1):
+            rs_step(d, d, sub, False)
+    if split:
+        swap.wait()
+        pair_sums(peer, 1)
+    for sub in (2, 3):
+        for d in (0, 1):
+            rs_step(d, 1 - d, sub, False)
+
+    piece = math.gcd(half_rows if split else rows, VB)
     blocks = half_width // VB
     for q in range(rows // piece):
-        row = pl.multiple_of(p * rows + q * piece, piece)
-        k = row // width
-        a = row % width
+        if split:
+            far = q * piece // half_rows
+            row = p * half_rows + q * piece - far * half_rows
+            k = row // half_width
+            a = row % half_width + (1 - v if far else v) * half_width
+        else:
+            row = p * rows + q * piece
+            k = row // width
+            a = row % width
         j = jnp.int32(0)
         i = jnp.int32(0)
         for m in range(pair_total):
@@ -165,7 +189,7 @@
             i = i + same * pair_i[m]
         eps_a = virt[domain[a // VB, i]]
         turned[...] = jnp.broadcast_to(eps_a, (VB, VB)).T
-        column = turned[pl.ds(pl.multiple_of(row % VB, piece), piece), :]
+        column = turned[pl.ds(pl.multiple_of(a % VB, piece), piece), :]
         for h in range(blocks):
             eps_b = virt[domain[v * blocks + h, j]]
             denominator = (column + eps_b) - occ_energy[i] - occ_energy[j]
@@ -221,12 +245,9 @@
     def mul(a, b):
         return jnp.dot(a, b, preferred_element_type=F32)
 
-    def half_of(k, side):
-        return amp[pl.ds(pl.multiple_of(k * width + side * half_width, half_width), half_width), :]
-
     def pair_product(k):
         i = pair_i[k]
-        return mul(own[i], half_of(k, v)) + mul(peer[i], half_of(k, 1 - v))
+        return mul(own[i], amp[half_at(k, 0), :]) + mul(peer[i], amp[half_at(k, 1), :])
 
     for e in range(extras):
         second[e] = pair_product(nocc + e)

time: 69.9 us -> 67.4 us (0.964)
  Pallas kernels: 64.5 us -> 62 us
    pallas_call x1, Pallas kernels: 64.5 us -> 62 us  [on_device(): pl.pallas_call(functools.partial(kernel, aux_count, occ_count, pair_total...]
where the time goes in v3:
time: 67.4 us; the launch traced here: 67.2 us
  Pallas kernels  62 us (92%)
  local copies, waits for them, and re-layouts  5.21 us (8%)
    pallas_call x1, Pallas kernels, on_device(): pl.pallas_call(functools.partial(kernel, aux_count, occ_count, pair_total...  62 us
    transpose x1, local copies, waits for them, and re-layouts, on_device(): return jnp.transpose(gamma, (1, 0, 2))  2.61 us
    unnamed x1, local copies, waits for them, and re-layouts  2.6 us

profile of v3, /device:TPU:0, one launch (start us, length us, event | category | flops | bytes accessed | tf_op | source)
XLA Modules:
  0.0 67.2 jit_solution(14393971698290604261)
XLA Ops:
  0.0 2.6 %copy.10 = bf16[312,8,256]{2,0,1:T(8,128)(2,1)} copy(bf16[312,8,256]{2,1,0:T(8,128)(2,1)} %param.6) | data formatting | bytes 2555904 | tf_op args[0]
  2.6 62.0 %shard_map.64 = bf16[8,312,256]{2,1,0:T(8,128)(2,1)} custom-call(s32[2,8]{1,0:T(2,128)} %bitcast.11, s32[4,8]{1,0:T(4,128)} %bitcast.10, s32[8]{0:T(128)} %count.1, f32[8]{0:T(128)} %occ_energy.1, f32[240,1,128]{2,1,0:T(1,128)} %bitcast.9, bf16[8,312,256]{2,1,0:T(8,128)(2,1)} %bitcast.8), custom_call_target="tpu_custom_call" | custom-call | tf_op jit(solution)/shard_map/pallas_call | solution.py:286
  64.6 2.6 %copy.8 = bf16[312,8,256]{2,1,0:T(8,128)(2,1)} copy(bf16[312,8,256]{2,0,1:T(8,128)(2,1)} %bitcast.7) | data formatting | bytes 2555904 | tf_op jit(solution)/shard_map/transpose | solution.py:313

commit v4 on v3

--- a/solution.py
+++ b/solution.py
@@ -58,7 +58,7 @@
     aux_count, occ_count, pair_total,
     partners, domain, count, occ_energy, virt, own,
     out,
-    peer, sums, amp, sent, came, turned, scale, second,
+    peer, sums, amp, sent, came, turned, scale, products,
     peer_sem, rs_send, rs_recv, ag_send, ag_recv,
 ):
     nocc, aux_rows, half_width = own.shape
@@ -118,7 +118,7 @@
 
     def half_at(k, far):
         if split:
-            return pl.ds((far * pair_total + k) * half_width, half_width)
+            return pl.ds(pl.multiple_of((far * pair_total + k) * half_width, half_width), half_width)
         side = 1 - v if far else v
         return pl.ds(pl.multiple_of(k * width + side * half_width, half_width), half_width)
 
@@ -238,23 +238,38 @@
             ag_copy(d, H - 2, sub).wait_recv()
             if sub in FIRST[d]:
                 ag_copy(d, H - 1, sub).start()
+    def mul(a, b):
+        return jnp.dot(a, b, preferred_element_type=F32)
+
+    def pair_product(k):
+        i = jnp.int32(0)
+        for m in range(pair_total):
+            i = i + (k == m).astype(jnp.int32) * pair_i[m]
+        return mul(own[i], amp[half_at(k, 0), :]) + mul(peer[i], amp[half_at(k, 1), :])
+
+    late = pair_total
+    start = 0
+    if split:
+        step = math.gcd(half_rows, half_width)
+        late = (half_width - step + half_rows - 1) // half_width + 1
+        start = lax.rem(p + H, N) * half_rows // half_width
+
+    def do_pair(n):
+        k = lax.rem(jnp.int32(start + n), pair_total)
+        products[k] = pair_product(k)
+
+    for n in range(late, pair_total):
+        do_pair(n)
     for d in (0, 1):
         for sub in FIRST[d]:
             ag_copy(d, H - 1, sub).wait_recv()
 
-    def mul(a, b):
-        return jnp.dot(a, b, preferred_element_type=F32)
-
-    def pair_product(k):
-        i = pair_i[k]
-        return mul(own[i], amp[half_at(k, 0), :]) + mul(peer[i], amp[half_at(k, 1), :])
-
-    for e in range(extras):
-        second[e] = pair_product(nocc + e)
+    for n in range(late):
+        do_pair(n)
     for j in range(nocc):
-        value = pair_product(j)
+        value = products[j]
         for e in range(extras):
-            value = value + second[e] * holds(j, e).astype(F32)
+            value = value + products[nocc + e] * holds(j, e).astype(F32)
         out[j] = value.astype(BF16)
 
     for d in (0, 1):
@@ -296,7 +311,7 @@
             pltpu.VMEM((2, H, rows, half_width), BF16),
             pltpu.VMEM((VB, VB), F32),
             pltpu.VMEM((rows, half_width), F32),
-            pltpu.VMEM((pair_total - nocc, aux_rows, half_width), F32),
+            pltpu.VMEM((pair_total, aux_rows, half_width), F32),
             pltpu.SemaphoreType.DMA((2,)),
             pltpu.SemaphoreType.DMA((2, H, SUBS)),
             pltpu.SemaphoreType.DMA((2, H, SUBS)),

time: 67.4 us -> 67.3 us (level)
  no operation moved by 1% of the time
where the time goes in v4:
time: 67.3 us; the launch traced here: 67.1 us
  Pallas kernels  61.9 us (92%)
  local copies, waits for them, and re-layouts  5.21 us (8%)
    pallas_call x1, Pallas kernels, on_device(): pl.pallas_call(functools.partial(kernel, aux_count, occ_count, pair_total...  61.9 us
    transpose x1, local copies, waits for them, and re-layouts, on_device(): return jnp.transpose(gamma, (1, 0, 2))  2.61 us
    unnamed x1, local copies, waits for them, and re-layouts  2.6 us

profile of v4, /device:TPU:0, one launch (start us, length us, event | category | flops | bytes accessed | tf_op | source)
XLA Modules:
  0.0 67.1 jit_solution(5029773418282872080)
XLA Ops:
  0.0 2.6 %copy.10 = bf16[312,8,256]{2,0,1:T(8,128)(2,1)} copy(bf16[312,8,256]{2,1,0:T(8,128)(2,1)} %param.6) | data formatting | bytes 2555904 | tf_op args[0]
  2.6 61.9 %shard_map.64 = bf16[8,312,256]{2,1,0:T(8,128)(2,1)} custom-call(s32[2,8]{1,0:T(2,128)} %bitcast.11, s32[4,8]{1,0:T(4,128)} %bitcast.10, s32[8]{0:T(128)} %count.1, f32[8]{0:T(128)} %occ_energy.1, f32[240,1,128]{2,1,0:T(1,128)} %bitcast.9, bf16[8,312,256]{2,1,0:T(8,128)(2,1)} %bitcast.8), custom_call_target="tpu_custom_call" | custom-call | tf_op jit(solution)/shard_map/pallas_call | solution.py:301
  64.5 2.6 %copy.8 = bf16[312,8,256]{2,1,0:T(8,128)(2,1)} copy(bf16[312,8,256]{2,0,1:T(8,128)(2,1)} %bitcast.7) | data formatting | bytes 2555904 | tf_op jit(solution)/shard_map/transpose | solution.py:328

commit v5 on v4

--- a/solution.py
+++ b/solution.py
@@ -319,7 +319,8 @@
             pltpu.SemaphoreType.DMA((2, H, SUBS)),
         ],
         compiler_params=pltpu.CompilerParams(
-            collective_id=0, has_side_effects=True, vmem_limit_bytes=56 * 1024 * 1024
+            collective_id=0, has_side_effects=True, vmem_limit_bytes=56 * 1024 * 1024,
+            allow_input_fusion=[False] * 5 + [True],
         ),
     )(
         partners.T, domain.T, pair_count, occ_energy,

time: 67.3 us -> 67.3 us (level)
  no operation moved by 1% of the time
where the time goes in v5:
time: 67.3 us; the launch traced here: 67.1 us
  Pallas kernels  61.9 us (92%)
  local copies, waits for them, and re-layouts  5.21 us (8%)
    pallas_call x1, Pallas kernels, on_device(): pl.pallas_call(functools.partial(kernel, aux_count, occ_count, pair_total...  61.9 us
    transpose x1, local copies, waits for them, and re-layouts, on_device(): return jnp.transpose(gamma, (1, 0, 2))  2.61 us
    unnamed x1, local copies, waits for them, and re-layouts  2.6 us

profile of v5, /device:TPU:0, one launch (start us, length us, event | category | flops | bytes accessed | tf_op | source)
XLA Modules:
  0.0 67.1 jit_solution(5029773418282872080)
XLA Ops:
  0.0 2.6 %copy.10 = bf16[312,8,256]{2,0,1:T(8,128)(2,1)} copy(bf16[312,8,256]{2,1,0:T(8,128)(2,1)} %param.6) | data formatting | bytes 2555904 | tf_op args[0]
  2.6 61.9 %shard_map.64 = bf16[8,312,256]{2,1,0:T(8,128)(2,1)} custom-call(s32[2,8]{1,0:T(2,128)} %bitcast.11, s32[4,8]{1,0:T(4,128)} %bitcast.10, s32[8]{0:T(128)} %count.1, f32[8]{0:T(128)} %occ_energy.1, f32[240,1,128]{2,1,0:T(1,128)} %bitcast.9, bf16[8,312,256]{2,1,0:T(8,128)(2,1)} %bitcast.8), custom_call_target="tpu_custom_call" | custom-call | tf_op jit(solution)/shard_map/pallas_call | solution.py:301
  64.5 2.6 %copy.8 = bf16[312,8,256]{2,1,0:T(8,128)(2,1)} copy(bf16[312,8,256]{2,0,1:T(8,128)(2,1)} %bitcast.7) | data formatting | bytes 2555904 | tf_op jit(solution)/shard_map/transpose | solution.py:329
